TPU v7x, 256 devices: a whole 4x4x8 slice. The times are simulated.
256 devices in a mesh: dp: 2 (over x_hi), expert: 2 (over core), ff: 32 (over z, y), mp: 2 (over x_lo).
Axes of the slice: x: 4 (x_hi: 2, x_lo: 2; x = x_hi * 2 + x_lo), y: 4, z: 8, core: 2. Of those that a mesh axis runs over, the one named last changes fastest.
Arguments:
- grad_tokens: bfloat16 [2, 1024, 3072], P('dp', ('expert', 'ff'), 'mp'), may hold values from -6 to 6
- routes: int32 [2, 1024, 2], P('dp', ('expert', 'ff')), may hold values from 0 to 1, all different within a row; in each aligned block of 16 rows (0 to 15, 16 to 31, ..., all dimensions but the last counted through in order) at most 16 rows name the same one
- gates: float32 [2, 1024, 2], P('dp', ('expert', 'ff')), may hold values from 0.1 to 1
- hidden_act: bfloat16 [2, 2, 1024, 8192], P('dp', 'expert', None, 'ff'), may hold values from -0.59765625 to 0.59765625
- weight: bfloat16 [2, 8192, 3072], P('expert', 'ff', 'mp'), may hold values from -0.0625 to 0.0625
Outputs:
- grad_hidden: bfloat16 [2, 2, 1024, 8192], P('dp', 'expert', 'mp', 'ff')
- grad_weight: float32 [2, 8192, 3072], P('expert', 'ff', ('mp', 'dp'))
Inputs may be any that keep to these rules, and one draw needn't show every extreme that they name: The 16 tokens of one device send at most 16 routes to one expert, and some device sends exactly 16; a token's two experts differ.
All inputs are finite; a program needn't handle non-finite values.
Results may differ from a plain program's by a relative error of at most 0.011.
Values may be sent and summed in bfloat16 or wider, within the bound.
A program may use at most 64 MiB of HBM per device.

v0:
```python
import jax
import jax.numpy as jnp
from jax import lax
from jax.sharding import PartitionSpec as P


def body(grad_tokens, routes, gates, hidden_act, weight):
    n_expert = lax.axis_size("expert")
    n_ffdev = lax.axis_size("ff")
    n_mpdev = lax.axis_size("mp")
    tok_dev = grad_tokens.shape[1]
    width_mp = grad_tokens.shape[2]
    capacity = hidden_act.shape[2]
    slot_count = capacity // (n_expert * n_ffdev)
    route_ids = routes.reshape(tok_dev * 2)
    expert_ids = jnp.arange(n_expert, dtype=jnp.int32)
    one_hot = (route_ids[:, None] == expert_ids[None, :]).astype(jnp.int32)
    slot_index = jnp.sum((jnp.cumsum(one_hot, axis=0) - 1) * one_hot, axis=1)
    target = route_ids * slot_count + slot_index
    slot_ids = jnp.arange(n_expert * slot_count, dtype=jnp.int32)
    placing = (slot_ids[:, None] == target[None, :]).astype(jnp.bfloat16)
    scaled = (grad_tokens[0][:, None, :].astype(jnp.float32) * gates[0][:, :, None]).astype(
        jnp.bfloat16
    )
    scaled = scaled.reshape(tok_dev * 2, width_mp)
    outgoing = jnp.dot(placing, scaled, preferred_element_type=jnp.float32).astype(jnp.bfloat16)
    outgoing = outgoing.reshape(n_expert, slot_count, width_mp)
    copies = jnp.broadcast_to(outgoing[:, None], (n_expert, n_ffdev, slot_count, width_mp))
    copies = copies.reshape(n_expert * n_ffdev, slot_count, width_mp)
    arrived = lax.all_to_all(copies, ("expert", "ff"), split_axis=0, concat_axis=0, tiled=True)
    routed = arrived.reshape(capacity, width_mp)
    weight_local = weight[0]
    grad_rows = lax.psum_scatter(
        lax.dot_general(
            routed, weight_local, (((1,), (1,)), ((), ())), preferred_element_type=jnp.float32
        ).astype(jnp.bfloat16),
        "mp",
        scatter_dimension=0,
        tiled=True,
    ).astype(jnp.float32)
    grad_hidden = grad_rows.astype(jnp.bfloat16).reshape(
        1, 1, capacity // n_mpdev, grad_rows.shape[1]
    )
    saved = hidden_act[0, 0]
    partial_grad = lax.dot_general(
        saved, routed, (((0,), (0,)), ((), ())), preferred_element_type=jnp.float32
    )
    grad_weight = lax.psum_scatter(
        partial_grad.astype(jnp.bfloat16), "dp", scatter_dimension=1, tiled=True
    ).astype(jnp.float32)
    return (grad_hidden, grad_weight.reshape(1, grad_weight.shape[0], grad_weight.shape[1]))


def solution(mesh):
    in_specs = (
        P("dp", ("expert", "ff"), "mp"),
        P("dp", ("expert", "ff"), None),
        P("dp", ("expert", "ff"), None),
        P("dp", "expert", None, "ff"),
        P("expert", "ff", "mp"),
    )
    out_specs = (P("dp", "expert", "mp", "ff"), P("expert", "ff", ("mp", "dp")))
    return jax.shard_map(body, mesh=mesh, in_specs=in_specs, out_specs=out_specs, check_vma=False)
```

profile of v0, /device:TPU:1, one launch (start us, length us, event | category | flops | bytes accessed | tf_op | source)
XLA Modules:
  0.0 151.0 jit_solution(10378857979981529857)
XLA Ops:
  7.2 0.0 copy-start
  7.2 0.0 reduce-scatter.5.cloned.1.call-start
  7.2 0.8 copy.10
  8.0 0.1 reshape.46
  8.1 0.8 copy.11
  8.9 0.1 mul.36
  9.0 0.1 fusion.4
  9.1 0.1 reduce_window_sum.11
  9.1 0.2 select_reduce_fusion
  9.3 0.8 bitcast_convert_fusion.1
  10.1 0.1 mul.34
  10.2 0.1 mul.35
  10.3 0.2 convolution_convert_fusion.1
  10.5 0.4 broadcast_in_dim.5
  10.9 0.0 copy-start.2
  10.9 86.2 %all_to_all.5 = bf16[64,16,1536]{2,1,0:T(8,128)(2,1)S(1)} all-to-all(bf16[64,16,1536]{2,1,0:T(8,128)(2,1)S(1)} %bitcast.20), channel_id=1, replica_groups=mesh['dp'=2,'expert'=2,'ff'=32,'mp'=2] {'expert','ff'}, dimensions={0} | all-to-all | bytes 6291456 | tf_op jit(solution)/shard_map/all_to_all | solution.py:30
  97.2 0.0 copy-start.1
  97.2 1.7 %copy-done.1 = bf16[64,16,1536]{2,1,0:T(8,128)(2,1)} copy-done((bf16[64,16,1536]{2,1,0:T(8,128)(2,1)}, bf16[64,16,1536]{2,1,0:T(8,128)(2,1)S(1)}, u32[]{:S(2)}) %copy-start.1) | copy-done | bytes 3145752
  98.8 0.0 copy-done.2
  98.8 1.9 %fusion = bf16[256,1536]{0,1:T(8,128)(2,1)} fusion(bf16[1024,1536]{1,0:T(8,128)(2,1)S(1)} %bitcast.21, bf16[1,1,1024,256]{3,2,1,0:T(8,128)(2,1)S(1)} %copy-done.2), kind=kOutput, calls=%fused_computation.1 | convolution fusion | flops 805699584 | bytes 4456448 | tf_op jit(solution)/shard_map/dot_general | solution.py:45
  100.8 0.0 reduce-scatter.5.cloned.1.call-update
  100.8 0.0 reduce-scatter.3.cloned.1.call-start
  100.8 0.0 copy-done
  100.8 3.7 %convolution_convert_fusion.2 = bf16[1024,256]{1,0:T(8,128)(2,1)} fusion(bf16[1024,1536]{1,0:T(8,128)(2,1)} %bitcast.22, bf16[1,256,1536]{2,1,0:T(8,128)(2,1)S(1)} %copy-done), kind=kOutput, calls=%fused_computation.3 | convolution fusion | flops 805568512 | bytes 4456448 | tf_op jit(solution)/shard_map/dot_general | solution.py:34
  104.5 0.0 reduce-scatter.3.cloned.1.call-update
  104.5 17.3 %reduce-scatter.5.cloned.1.call-done = bf16[256,768]{0,1:T(8,128)(2,1)} async-done(((bf16[256,1536]{0,1:T(8,128)(2,1)}), bf16[256,768]{0,1:T(8,128)(2,1)}) %reduce-scatter.5.cloned.1.call-update) | async-done | bytes 393232 | tf_op jit(solution)/shard_map/reduce_scatter | solution.py:48
  121.8 1.0 bitcast_convert_fusion
  122.9 1.1 copy.12
  124.0 20.2 %reduce-scatter.3.cloned.1.call-done = bf16[512,256]{1,0:T(8,128)(2,1)} async-done(((bf16[1024,256]{1,0:T(8,128)(2,1)}), bf16[512,256]{1,0:T(8,128)(2,1)}) %reduce-scatter.3.cloned.1.call-update) | async-done | bytes 262160 | tf_op jit(solution)/shard_map/reduce_scatter | solution.py:33
  (1 shorter events, 0.0 us)
Async XLA Ops:
  7.2 93.7 %copy-start = (bf16[1,256,1536]{2,1,0:T(8,128)(2,1)S(1)}, bf16[1,256,1536]{2,1,0:T(8,128)(2,1)}, u32[]{:S(2)}) copy-start(bf16[1,256,1536]{2,1,0:T(8,128)(2,1)} %param.9) | copy-start | bytes 2359300
  7.2 114.6 %reduce-scatter.5.cloned.1.call-start = ((), (), s32[]{:S(2)}) async-start(), calls=%async_computation.4 | async-start | bytes 1179648 | tf_op jit(solution)/shard_map/reduce_scatter | solution.py:48
  10.9 87.9 %copy-start.2 = (bf16[1,1,1024,256]{3,2,1,0:T(8,128)(2,1)S(1)}, bf16[1,1,1024,256]{3,2,1,0:T(8,128)(2,1)}, u32[]{:S(2)}) copy-start(bf16[1,1,1024,256]{3,2,1,0:T(8,128)(2,1)} %param.8) | copy-start | bytes 1572868
  97.2 1.7 %copy-start.1 = (bf16[64,16,1536]{2,1,0:T(8,128)(2,1)}, bf16[64,16,1536]{2,1,0:T(8,128)(2,1)S(1)}, u32[]{:S(2)}) copy-start(bf16[64,16,1536]{2,1,0:T(8,128)(2,1)S(1)} %all_to_all.5) | copy-start | bytes 9437188
  100.8 43.4 %reduce-scatter.3.cloned.1.call-start = ((), (), s32[]{:S(2)}) async-start(), calls=%async_computation.3 | async-start | bytes 786432 | tf_op jit(solution)/shard_map/reduce_scatter | solution.py:33
Sparse Core Ops, SparseCore 0:
  100.9 20.8 reduce-scatter.4
  125.0 19.1 reduce-scatter.2
where the time goes:
time: 151 us
  blocking collectives  86.2 us (57%)
  waiting for transfers between devices  37.5 us (25%)
  between operations  14.1 us (9%)
  matrix products  5.82 us (4%)
  local copies, waits for them, and re-layouts  5.16 us (3%)
  other arithmetic  2.17 us (1%)
    all_to_all x1, blocking collectives, body(): lax.all_to_all(copies, ('expert', 'ff'), split_axis=0, concat_axis=0, til...  86.2 us
    reduce_scatter x1, waiting for transfers between devices, body(): lax.psum_scatter(lax.dot_general(routed, weight_local, (((1,), (1,)), (()...  20.2 us
    reduce_scatter x1, waiting for transfers between devices, body(): lax.psum_scatter(partial_grad.astype(jnp.bfloat16), 'dp', scatter_dimensi...  17.3 us
    unnamed x9, local copies, waits for them, and re-layouts  4.41 us
    dot_general x1, matrix products, body(): lax.dot_general(routed, weight_local, (((1,), (1,)), ((), ())), preferred...  3.69 us
  transfers between devices with their start and end apart: 2, of which 2 were waited for; matrix products, arithmetic and copies ran while one was open for 4% of the time, Pallas kernels for 0%

commit v1 on v0

v1 whole, which is shorter than its diff:
```python
import jax
import jax.numpy as jnp
from jax import lax
from jax.experimental import pallas as pl
from jax.experimental.pallas import tpu as pltpu
from jax.sharding import PartitionSpec as P

MESH = pl.DeviceIdType.MESH
NY, NZ = 4, 8
GATE = 128
FIRST = 640
YS = (1, 3, 2)
NEAR = (2, -2, 1, -1)
PAIRS = ((0, 1), (-1, 2), (-2, 3), (-3, 4))
DIST = (0, 1, -1, 2, -2, 3, -3, 4)


def kernel(tok_hbm, gate_ref, route_ref, hid_hbm, w_hbm, gh_ref, keep_hbm, got_hbm,
           rows, hid, w, acc_s, acc_k, gh_keep, gh_send, gh_got, gw_send, gw_got, in_sem, out_sem, send_sem, recv_sem):
    dp, e, f, mp = (lax.axis_index(a) for a in ("dp", "expert", "ff", "mp"))
    y, z = lax.rem(f, NY), f // NY
    width = w.shape[1]
    half = width // 2

    def dev(dy=0, dz=0):
        return (dp, e, lax.rem(z + dz + NZ, NZ) * NY + lax.rem(y + dy + NY, NY), mp)

    def plane(d):
        return lax.rem(z + d + NZ, NZ)

    sibling, across, pair = (dp, 1 - e, f, mp), (1 - dp, e, f, mp), (dp, e, f, 1 - mp)
    loads = [
        pltpu.make_async_copy(tok_hbm, rows.at[e, z, y, :, pl.ds(0, width)], in_sem.at[0]),
        pltpu.make_async_copy(hid_hbm, hid, in_sem.at[1]),
        pltpu.make_async_copy(w_hbm, w, in_sem.at[2]),
    ]
    loads[0].start()
    barrier = pltpu.get_barrier_semaphore()
    partners = [dev(dy=k) for k in YS] + [dev(dz=d) for d in NEAR] + [sibling, across, pair]
    for p in partners:
        pl.semaphore_signal(barrier, inc=1, device_id=p, device_id_type=MESH)
    for load in loads[1:]:
        load.start()

    tok = rows.shape[3]
    diag = lax.broadcasted_iota(jnp.int32, (tok, tok), 0) == lax.broadcasted_iota(jnp.int32, (tok, tok), 1)
    lane = lax.broadcasted_iota(jnp.int32, (tok, GATE), 1)
    block = jnp.zeros((tok, GATE), jnp.float32)
    for expert in range(2):
        mine = jnp.sum(jnp.where(route_ref[...] == expert, gate_ref[...], 0.0), axis=0, keepdims=True)
        col = jnp.sum(jnp.where(diag, jnp.broadcast_to(mine, (tok, tok)), 0.0), axis=1, keepdims=True)
        high = col.astype(jnp.bfloat16).astype(jnp.float32)
        block = jnp.where(lane == 2 * expert, high, jnp.where(lane == 2 * expert + 1, col - high, block))
    rows[e, z, y, :, pl.ds(width, GATE)] = block.astype(jnp.bfloat16)
    acc_s[...] = jnp.zeros_like(acc_s)
    acc_k[...] = jnp.zeros_like(acc_k)
    loads[0].wait()
    pl.semaphore_wait(barrier, len(partners))

    sent, count = [], [0]

    def send(src, dst, to):
        i = count[0]
        count[0] += 1
        copy = pltpu.make_async_remote_copy(
            src_ref=src, dst_ref=dst, send_sem=send_sem.at[i], recv_sem=recv_sem.at[i], device_id=to, device_id_type=MESH
        )
        copy.start()
        sent.append(copy)
        return copy

    part_a, part_b = pl.ds(0, FIRST), pl.ds(FIRST, width + GATE - FIRST)

    def a_plane(d, dz):
        ref = rows.at[e, plane(d), :, :, part_a]
        return send(ref, ref, dev(dz=dz))

    def b_block(d, dy=0, dz=0):
        ref = rows.at[e, plane(d), y, :, part_b]
        return send(ref, ref, dev(dy=dy, dz=dz))

    a_own = rows.at[e, z, y, :, part_a]
    a_y = [send(a_own, a_own, dev(dy=k)) for k in YS]
    b_z = {-dz: b_block(0, dz=dz) for dz in NEAR}
    b_y = {0: [b_block(0, dy=k) for k in YS]}
    for copy in a_y:
        copy.wait_recv()
    a_z = {-dz: a_plane(0, dz) for dz in NEAR}
    b_z[-2].wait_recv()
    b_z[-3] = b_block(-2, dz=1)
    b_y[-2] = [b_block(-2, dy=k) for k in YS]
    b_z[2].wait_recv()
    b_z[3] = b_block(2, dz=-1)
    b_z[4] = b_block(2, dz=-2)
    b_y[2] = [b_block(2, dy=k) for k in YS]
    for d in (-1, 1):
        b_z[d].wait_recv()
        b_y[d] = [b_block(d, dy=k) for k in YS]
    a_z[-2].wait_recv()
    a_z[-3] = a_plane(-2, 1)
    a_z[4] = a_plane(-2, 2)
    a_z[2].wait_recv()
    a_z[3] = a_plane(2, -1)
    for d in (-3, 3, 4):
        b_z[d].wait_recv()
        b_y[d] = [b_block(d, dy=k) for k in YS]

    halves = {}

    def finish(d):
        if d in (1, -1, 3, -3, 4):
            a_z[d].wait_recv()
        for copy in b_y[d]:
            copy.wait_recv()
        ref = rows.at[e, plane(d)]
        halves[d] = send(ref, ref, sibling)

    off_s = pl.multiple_of((1 - dp) * half, half)
    off_k = pl.multiple_of(dp * half, half)
    gh_sends, gw_sends = [], []
    n_rows = NY * tok
    step = 256

    def compute(ds, last):
        places = [(c, plane(d)) for c in (mp, 1 - mp) for d in ds]

        def take(at):
            return jnp.concatenate([rows[c, p, :, :, at].reshape(n_rows, -1) for c, p in places], axis=0)

        gates = take(pl.ds(width, GATE)).astype(jnp.float32)
        lanes = lax.broadcasted_iota(jnp.int32, gates.shape, 1)
        g = jnp.sum(jnp.where((lanes // 2) == e, gates, 0.0), axis=1, keepdims=True)
        h = jnp.concatenate([hid[c, p] for c, p in places], axis=0)
        h = (h.astype(jnp.float32) * g).astype(jnp.bfloat16)

        def grow(acc, off, n):
            x = take(pl.ds(pl.multiple_of(off + n, 128), step))
            return acc[:, n:n + step] + lax.dot_general(h, x, (((0,), (0,)), ((), ())), preferred_element_type=jnp.float32)

        for i, n in enumerate(range(0, half, step)):
            total = grow(acc_s, off_s, n)
            if last:
                gw_send[i] = total.astype(jnp.bfloat16)
                gw_sends.append(send(gw_send.at[i], gw_got.at[i], across))
            else:
                acc_s[:, n:n + step] = total
        gh = lax.dot_general(take(pl.ds(0, width)), w[...], (((1,), (1,)), ((), ())), preferred_element_type=jnp.float32) * g
        for i, d in enumerate(ds):
            gh_keep[plane(d)] = gh[i * n_rows:(i + 1) * n_rows]
            j = i + len(ds)
            gh_send[plane(d)] = gh[j * n_rows:(j + 1) * n_rows].astype(jnp.bfloat16)
            gh_sends.append(send(gh_send.at[plane(d)], gh_got.at[plane(d)], pair))
        for n in range(0, half, step):
            acc_k[:, n:n + step] = grow(acc_k, off_k, n)

    finish(0)
    loads[1].wait()
    loads[2].wait()
    finish(1)
    finish(-1)
    finish(2)
    for i, ds in enumerate(PAIRS):
        for d in ds:
            halves[d].wait_recv()
        compute(ds, i == len(PAIRS) - 1)
        if i == 0:
            finish(-2)
            finish(3)
        if i == 1:
            finish(-3)
            finish(4)

    keep_out = pltpu.make_async_copy(acc_k, keep_hbm, out_sem.at[0])
    keep_out.start()
    for copy in gh_sends:
        copy.wait_recv()
    gh_ref[...] = (gh_keep[...] + gh_got[...].astype(jnp.float32)).astype(jnp.bfloat16)
    keep_out.wait()
    for copy in sent:
        copy.wait_send()
    outs = []
    for i, copy in enumerate(gw_sends):
        copy.wait_recv()
        out = pltpu.make_async_copy(gw_got.at[i], got_hbm.at[i], out_sem.at[i + 1])
        out.start()
        outs.append(out)
    for out in outs:
        out.wait()


def body(grad_tokens, routes, gates, hidden_act, weight):
    _, tok, width = grad_tokens.shape
    cap, ff = hidden_act.shape[2:]
    half, n_rows = width // 2, NY * tok
    pieces = half // 256
    n_copies = 3 + 4 + 3 + 7 + 3 * NZ + NZ + NZ + pieces
    vmem, hbm = pl.BlockSpec(memory_space=pltpu.VMEM), pl.BlockSpec(memory_space=pl.ANY)
    bf16, f32 = jnp.bfloat16, jnp.float32
    gh, keep, got = pl.pallas_call(
        kernel,
        out_shape=(
            jax.ShapeDtypeStruct((NZ, n_rows, ff), bf16),
            jax.ShapeDtypeStruct((ff, half), f32),
            jax.ShapeDtypeStruct((pieces, ff, 256), bf16),
        ),
        in_specs=[hbm, vmem, vmem, hbm, hbm],
        out_specs=(vmem, hbm, hbm),
        scratch_shapes=[
            pltpu.VMEM((2, NZ, NY, tok, width + GATE), bf16),
            pltpu.VMEM((2, NZ, n_rows, ff), bf16),
            pltpu.VMEM((ff, width), bf16),
            pltpu.VMEM((ff, half), f32),
            pltpu.VMEM((ff, half), f32),
            pltpu.VMEM((NZ, n_rows, ff), f32),
            pltpu.VMEM((NZ, n_rows, ff), bf16),
            pltpu.VMEM((NZ, n_rows, ff), bf16),
            pltpu.VMEM((pieces, ff, 256), bf16),
            pltpu.VMEM((pieces, ff, 256), bf16),
            pltpu.SemaphoreType.DMA((3,)),
            pltpu.SemaphoreType.DMA((1 + pieces,)),
            pltpu.SemaphoreType.DMA((n_copies,)),
            pltpu.SemaphoreType.DMA((n_copies,)),
        ],
        compiler_params=pltpu.CompilerParams(collective_id=0, has_side_effects=True, vmem_limit_bytes=32 * 2**20),
    )(
        grad_tokens[0],
        gates[0].T,
        routes[0].T,
        hidden_act.reshape(2, NZ, n_rows, ff),
        weight[0],
    )
    grad_hidden = gh.reshape(1, 1, cap // 2, ff)
    got = jnp.concatenate([got[i] for i in range(pieces)], axis=1)
    grad_weight = keep + got.astype(f32)
    return grad_hidden, grad_weight.reshape(1, ff, half)


def solution(mesh):
    in_specs = (
        P("dp", ("expert", "ff"), "mp"),
        P("dp", ("expert", "ff"), None),
        P("dp", ("expert", "ff"), None),
        P("dp", "expert", None, "ff"),
        P("expert", "ff", "mp"),
    )
    out_specs = (P("dp", "expert", "mp", "ff"), P("expert", "ff", ("mp", "dp")))
    return jax.shard_map(body, mesh=mesh, in_specs=in_specs, out_specs=out_specs, check_vma=False)
```

time: 151 us -> 49.4 us (0.33)
  blocking collectives: 86.2 us -> 0 us
  Pallas kernels: 0 us -> 43.1 us
  waiting for transfers between devices: 37.5 us -> 0 us
  between operations: 14.1 us -> 0.67 us
  matrix products: 5.82 us -> 0 us
    all_to_all x1 -> x0, blocking collectives: 86.2 us -> none  [body(): lax.all_to_all(copies, ('expert', 'ff'), split_axis=0, concat_axis=0, til...]
    pallas_call x0 -> x1, Pallas kernels: none -> 43.1 us  [body(): pl.pallas_call(kernel, out_shape=(jax.ShapeDtypeStruct((NZ, n_rows, ff),...]
    reduce_scatter x2 -> x0, waiting for transfers between devices: 37.4 us -> none  [the longest x1 20.2 us: body(): lax.psum_scatter(lax.dot_general(routed, weight_local, (((1,), (1,)), (()...]
    dot_general x3 -> x0, matrix products: 5.82 us -> none  [the longest x1 3.69 us: body(): lax.dot_general(routed, weight_local, (((1,), (1,)), ((), ())), preferred...]
    unnamed x9 -> x11, local copies, waits for them, and re-layouts: 4.41 us -> 4.35 us
  transfers between devices with their start and end apart: 2 -> 0, of which waited for: 2 -> 0; matrix products, arithmetic and copies ran while one was open for 4% -> 0% of each run, Pallas kernels for 0% -> 0%
where the time goes in v1:
time: 49.4 us; the launch traced here: 49.1 us
  Pallas kernels  43.1 us (87%)
  local copies, waits for them, and re-layouts  4.38 us (9%)
  other arithmetic  0.97 us (2%)
  between operations  0.67 us (1%)
    pallas_call x1, Pallas kernels, body(): pl.pallas_call(kernel, out_shape=(jax.ShapeDtypeStruct((NZ, n_rows, ff),...  43.1 us
    unnamed x11, local copies, waits for them, and re-layouts  4.35 us

profile of v1, /device:TPU:1, one launch (start us, length us, event | category | flops | bytes accessed | tf_op | source)
XLA Modules:
  0.0 49.1 jit_solution(1674380637513542012)
XLA Ops:
  0.6 0.0 copy-start.4
  0.6 0.0 copy-start.3
  0.7 0.7 %copy-done.4 = s32[1,16,2]{1,2,0:T(2,128)S(1)} copy-done((s32[1,16,2]{1,2,0:T(2,128)S(1)}, s32[1,16,2]{1,2,0:T(2,128)}, u32[]{:S(2)}) %copy-start.4) | copy-done | bytes 152
  1.3 0.0 copy-done.3
  1.3 0.0 copy-start
  1.3 1.1 %copy-done = bf16[1,256,1536]{2,1,0:T(8,128)(2,1)S(1)} copy-done((bf16[1,256,1536]{2,1,0:T(8,128)(2,1)S(1)}, bf16[1,256,1536]{2,1,0:T(8,128)(2,1)}, u32[]{:S(2)}) %copy-start) | copy-done | bytes 786456
  2.5 0.0 copy-start.1
  2.5 1.0 %copy-done.1 = bf16[1,1,1024,256]{3,2,1,0:T(8,128)(2,1)S(1)} copy-done((bf16[1,1,1024,256]{3,2,1,0:T(8,128)(2,1)S(1)}, bf16[1,1,1024,256]{3,2,1,0:T(8,128)(2,1)}, u32[]{:S(2)}) %copy-start.1) | copy-done | bytes 524312
  3.5 0.0 copy-start.2
  3.5 0.8 %copy-done.2 = bf16[1,16,1536]{2,1,0:T(8,128)(2,1)S(1)} copy-done((bf16[1,16,1536]{2,1,0:T(8,128)(2,1)S(1)}, bf16[1,16,1536]{2,1,0:T(8,128)(2,1)}, u32[]{:S(2)}) %copy-start.2) | copy-done | bytes 49176
  4.3 43.1 %shard_map.68 = (bf16[8,64,256]{2,1,0:T(8,128)(2,1)S(1)}, f32[256,768]{1,0:T(8,128)S(1)}, bf16[3,256,256]{2,1,0:T(8,128)(2,1)S(1)}) custom-call(bf16[16,1536]{1,0:T(8,128)(2,1)S(1)} %bitcast.21, f32[2,16]{1,0:T(2,128)S(1)} %bitcast.22, s32[2,16]{1,0:T(2,128)S(1)} %bitcast.23, bf16[2,8,64,256]{3,2,1,0:T(8,128)(2,1)S(1)} %bitcast.19, ...), custom_call_target="tpu_custom_call" | custom-call | tf_op jit(solution)/shard_map/pallas_call | solution.py:199
  47.4 1.0 %add_bitcast_fusion = f32[1,256,768]{2,1,0:T(8,128)} fusion(f32[256,768]{1,0:T(8,128)S(1)} %get-tuple-element.6, bf16[256,256]{1,0:T(8,128)(2,1)S(1)} %get-tuple-element.9, bf16[256,256]{1,0:T(8,128)(2,1)S(1)} %get-tuple-element.10, bf16[256,256]{1,0:T(8,128)(2,1)S(1)} %get-tuple-element.8), kind=kLoop, calls=%fused_computation | loop fusion | flops 1376256 | bytes 1966080 | tf_op jit(solution)/shard_map/reshape | solution.py:235
  48.4 0.7 %copy.8 = bf16[1,1,512,256]{3,2,1,0:T(8,128)(2,1)} copy(bf16[1,1,512,256]{3,2,1,0:T(8,128)(2,1)S(1)} %bitcast.20) | data formatting | bytes 524288
  (1 shorter events, 0.0 us)
Async XLA Ops:
  0.6 0.7 %copy-start.4 = (s32[1,16,2]{1,2,0:T(2,128)S(1)}, s32[1,16,2]{1,2,0:T(2,128)}, u32[]{:S(2)}) copy-start(s32[1,16,2]{1,2,0:T(2,128)} %param.6) | copy-start | bytes 388
  0.6 0.7 %copy-start.3 = (f32[1,16,2]{1,2,0:T(2,128)S(1)}, f32[1,16,2]{1,2,0:T(2,128)}, u32[]{:S(2)}) copy-start(f32[1,16,2]{1,2,0:T(2,128)} %param.7) | copy-start | bytes 388
  1.3 1.1 %copy-start = (bf16[1,256,1536]{2,1,0:T(8,128)(2,1)S(1)}, bf16[1,256,1536]{2,1,0:T(8,128)(2,1)}, u32[]{:S(2)}) copy-start(bf16[1,256,1536]{2,1,0:T(8,128)(2,1)} %param.9) | copy-start | bytes 2359300
  2.5 1.0 %copy-start.1 = (bf16[1,1,1024,256]{3,2,1,0:T(8,128)(2,1)S(1)}, bf16[1,1,1024,256]{3,2,1,0:T(8,128)(2,1)}, u32[]{:S(2)}) copy-start(bf16[1,1,1024,256]{3,2,1,0:T(8,128)(2,1)} %param.8) | copy-start | bytes 1572868
  3.5 0.8 %copy-start.2 = (bf16[1,16,1536]{2,1,0:T(8,128)(2,1)S(1)}, bf16[1,16,1536]{2,1,0:T(8,128)(2,1)}, u32[]{:S(2)}) copy-start(bf16[1,16,1536]{2,1,0:T(8,128)(2,1)} %param.5) | copy-start | bytes 147460

commit v2 on v0

v2 whole, which is shorter than its diff:
```python
import jax
import jax.numpy as jnp
from jax import lax
from jax.experimental import pallas as pl
from jax.experimental.pallas import tpu as pltpu
from jax.sharding import PartitionSpec as P

MESH = pl.DeviceIdType.MESH
NY, NZ = 4, 8
GATE = 128
SPLITS = (384, 256)
YS = (1, 3, 2)
NEAR = (2, -2, 1, -1)
PAIRS = ((0, 1), (-1, 2), (-2, 3), (-3, 4))
STEP = 256
N_COPIES = 2 * (3 + 4 + 3 + 7 + 3 * NZ + 2 * NZ) + NZ + 8


def kernel(tok_hbm, gate_hbm, route_hbm, hid_hbm, w_hbm, acc_k, gw_got, gh_keep, gh_got,
           gate_ref, route_ref, rows, hid, scaled, w, acc_s, gh_send, gw_send, in_sem, send_sem, recv_sem):
    dp, e, f, mp = (lax.axis_index(a) for a in ("dp", "expert", "ff", "mp"))
    y, z = lax.rem(f, NY), f // NY
    width = w.shape[1]
    half = width // 2

    def dev(dy=0, dz=0):
        return (dp, e, lax.rem(z + dz + NZ, NZ) * NY + lax.rem(y + dy + NY, NY), mp)

    def plane(d):
        return lax.rem(z + d + NZ, NZ)

    sibling, across, pair = (dp, 1 - e, f, mp), (1 - dp, e, f, mp), (dp, e, f, 1 - mp)

    off_s, off_k = pl.multiple_of((1 - dp) * half, half), pl.multiple_of(dp * half, half)
    at_s, at_k = pl.ds(GATE, half), pl.ds(GATE + half, half)
    own = rows.at[e, z, y]
    loads = [
        pltpu.make_async_copy(tok_hbm.at[:, pl.ds(off_s, half)], own.at[:, at_s], in_sem.at[0]),
        pltpu.make_async_copy(tok_hbm.at[:, pl.ds(off_k, half)], own.at[:, at_k], in_sem.at[1]),
        pltpu.make_async_copy(gate_hbm, gate_ref, in_sem.at[2]),
        pltpu.make_async_copy(route_hbm, route_ref, in_sem.at[3]),
    ]
    later = [
        pltpu.make_async_copy(hid_hbm, hid, in_sem.at[4]),
        pltpu.make_async_copy(w_hbm.at[:, pl.ds(off_s, half)], w.at[:, pl.ds(0, half)], in_sem.at[5]),
        pltpu.make_async_copy(w_hbm.at[:, pl.ds(off_k, half)], w.at[:, pl.ds(half, half)], in_sem.at[6]),
    ]
    for load in loads:
        load.start()
    barrier = pltpu.get_barrier_semaphore()
    partners = [dev(dy=k) for k in YS] + [dev(dz=d) for d in NEAR] + [sibling, across, pair]
    for p in partners:
        pl.semaphore_signal(barrier, inc=1, device_id=p, device_id_type=MESH)
    for load in later:
        load.start()
    acc_s[...] = jnp.zeros_like(acc_s)
    acc_k[...] = jnp.zeros_like(acc_k)

    tok = rows.shape[3]
    diag = lax.broadcasted_iota(jnp.int32, (tok, tok), 0) == lax.broadcasted_iota(jnp.int32, (tok, tok), 1)
    lane = lax.broadcasted_iota(jnp.int32, (tok, GATE), 1)
    block = jnp.zeros((tok, GATE), jnp.float32)
    loads[2].wait()
    loads[3].wait()
    for expert in range(2):
        mine = jnp.sum(jnp.where(route_ref[...] == expert, gate_ref[...], 0.0), axis=0, keepdims=True)
        col = jnp.sum(jnp.where(diag, jnp.broadcast_to(mine, (tok, tok)), 0.0), axis=1, keepdims=True)
        high = col.astype(jnp.bfloat16).astype(jnp.float32)
        block = jnp.where(lane == 2 * expert, high, jnp.where(lane == 2 * expert + 1, col - high, block))
    rows[e, z, y, :, pl.ds(0, GATE)] = block.astype(jnp.bfloat16)
    loads[0].wait()
    loads[1].wait()
    pl.semaphore_wait(barrier, len(partners))

    sent = []

    def send(src, dst, to):
        i = len(sent)
        copy = pltpu.make_async_remote_copy(
            src_ref=src, dst_ref=dst, send_sem=send_sem.at[i], recv_sem=recv_sem.at[i], device_id=to, device_id_type=MESH
        )
        copy.start()
        sent.append(copy)
        return copy

    def wait(copies):
        for copy in copies:
            copy.wait_recv()

    class Gather:
        def __init__(self, start, size, first):
            self.a, self.b = pl.ds(start, first), pl.ds(start + first, size - first)
            self.sib = {}

        def a_plane(self, d, dz):
            ref = rows.at[e, plane(d), :, :, self.a]
            return send(ref, ref, dev(dz=dz))

        def b_block(self, d, dy=0, dz=0):
            ref = rows.at[e, plane(d), y, :, self.b]
            return send(ref, ref, dev(dy=dy, dz=dz))

        def spread(self, d):
            self.b_y[d] = [self.b_block(d, dy=k) for k in YS]

        def start(self):
            ref = rows.at[e, z, y, :, self.a]
            self.a_y = [send(ref, ref, dev(dy=k)) for k in YS]
            self.b_z = {-dz: self.b_block(0, dz=dz) for dz in NEAR}
            self.b_y = {}
            self.spread(0)

        def a_near(self):
            wait(self.a_y)
            self.a_z = {-dz: self.a_plane(0, dz) for dz in NEAR}

        def b_far(self):
            self.b_z[-2].wait_recv()
            self.b_z[-3] = self.b_block(-2, dz=1)
            self.spread(-2)
            self.b_z[2].wait_recv()
            self.b_z[3] = self.b_block(2, dz=-1)
            self.b_z[4] = self.b_block(2, dz=-2)
            self.spread(2)
            for d in (-1, 1):
                self.b_z[d].wait_recv()
                self.spread(d)

        def a_far(self):
            self.a_z[-2].wait_recv()
            self.a_z[-3] = self.a_plane(-2, 1)
            self.a_z[4] = self.a_plane(-2, 2)
            self.a_z[2].wait_recv()
            self.a_z[3] = self.a_plane(2, -1)

        def b_last(self):
            for d in (-3, 3, 4):
                self.b_z[d].wait_recv()
                self.spread(d)

        def share_a(self, ds):
            for d in ds:
                if d not in (0, 2, -2):
                    self.a_z[d].wait_recv()
                ref = rows.at[e, plane(d), :, :, self.a]
                self.sib.setdefault(d, []).append(send(ref, ref, sibling))

        def share_b(self, ds):
            for d in ds:
                wait(self.b_y[d])
                ref = rows.at[e, plane(d), :, :, self.b]
                self.sib.setdefault(d, []).append(send(ref, ref, sibling))

    n_rows = NY * tok
    gh_sends, gw_sends = [], []

    def take(ds, at):
        parts = [rows[c, plane(d), :, :, at].reshape(n_rows, -1) for c in (mp, 1 - mp) for d in ds]
        return jnp.concatenate(parts, axis=0)

    def gate_of(ds):
        gates = take(ds, pl.ds(0, GATE)).astype(jnp.float32)
        lanes = lax.broadcasted_iota(jnp.int32, gates.shape, 1)
        return jnp.sum(jnp.where((lanes // 2) == e, gates, 0.0), axis=1, keepdims=True)

    def grow(i, ds, acc, start, n):
        x = take(ds, pl.ds(start + n, STEP))
        more = lax.dot_general(scaled[i], x, (((0,), (0,)), ((), ())), preferred_element_type=jnp.float32)
        return acc[:, n:n + STEP] + more

    def compute_s(i):
        ds = PAIRS[i]
        for d in ds:
            wait(first.sib[d])
        h = jnp.concatenate([hid[c, plane(d)] for c in (mp, 1 - mp) for d in ds], axis=0)
        scaled[i] = (h.astype(jnp.float32) * gate_of(ds)).astype(jnp.bfloat16)
        for n in range(0, half, STEP):
            total = grow(i, ds, acc_s, GATE, n)
            if i == len(PAIRS) - 1:
                at = pl.ds(n, STEP)
                gw_send[:, n:n + STEP] = total.astype(jnp.bfloat16)
                gw_sends.append(send(gw_send.at[:, at], gw_got.at[:, at], across))
            else:
                acc_s[:, n:n + STEP] = total

    def compute_k(i):
        ds = PAIRS[i]
        for d in ds:
            wait(second.sib[d])
        x = take(ds, pl.ds(GATE, width))
        gh = lax.dot_general(x, w[...], (((1,), (1,)), ((), ())), preferred_element_type=jnp.float32) * gate_of(ds)
        for j, d in enumerate(ds):
            gh_send[plane(d)] = gh[(j + 2) * n_rows:(j + 3) * n_rows].astype(jnp.bfloat16)
            gh_sends.append(send(gh_send.at[plane(d)], gh_got.at[plane(d)], pair))
            gh_keep[plane(d)] = gh[j * n_rows:(j + 1) * n_rows]
        for n in range(0, half, STEP):
            acc_k[:, n:n + STEP] = grow(i, ds, acc_k, GATE + half, n)

    first, second = Gather(0, GATE + half, SPLITS[0]), Gather(GATE + half, half, SPLITS[1])
    first.start()
    first.a_near()
    first.b_far()
    second.start()
    first.share_a((0,))
    first.share_b((0,))
    first.a_far()
    first.b_last()
    first.share_a((-2, 2, -1, 1))
    first.share_b((-2, 2, -1, 1))
    second.a_near()
    second.b_far()
    later[0].wait()
    compute_s(0)
    compute_s(1)
    second.share_a((0,))
    second.share_b((0,))
    first.share_a((-3, 3, 4))
    first.share_b((-3, 3, 4))
    second.a_far()
    second.b_last()
    second.share_a((-2, 2, -1, 1))
    second.share_b((-2, 2, -1, 1))
    compute_s(2)
    compute_s(3)
    later[1].wait()
    later[2].wait()
    compute_k(0)
    compute_k(1)
    second.share_a((-3, 3, 4))
    second.share_b((-3, 3, 4))
    compute_k(2)
    compute_k(3)
    for copy in sent:
        copy.wait_send()
    wait(gh_sends)
    wait(gw_sends)


def finish(acc_k, gw_got, gh_keep, gh_got, gh_hbm, gw_hbm, gh, gw, sem):
    gh[...] = (gh_keep[...] + gh_got[...].astype(jnp.float32)).astype(jnp.bfloat16)
    outs = [pltpu.make_async_copy(gh, gh_hbm, sem.at[0])]
    outs[0].start()
    n = gw.shape[0] // 4
    for i in range(4):
        at = pl.ds(i * n, n)
        gw[at] = acc_k[at] + gw_got[at].astype(jnp.float32)
        outs.append(pltpu.make_async_copy(gw.at[at], gw_hbm.at[at], sem.at[i + 1]))
        outs[-1].start()
    for out in outs:
        out.wait()


def body(grad_tokens, routes, gates, hidden_act, weight):
    _, tok, width = grad_tokens.shape
    cap, ff = hidden_act.shape[2:]
    half, n_rows = width // 2, NY * tok
    vmem, hbm = pl.BlockSpec(memory_space=pltpu.VMEM), pl.BlockSpec(memory_space=pltpu.HBM)
    bf16, f32 = jnp.bfloat16, jnp.float32
    operands = (
        grad_tokens[0],
        gates[0].T,
        routes[0].T,
        hidden_act.reshape(2, NZ, n_rows, ff),
        weight[0],
    )
    halves = pl.pallas_call(
        kernel,
        out_shape=(
            pltpu.VMEM((ff, half), f32),
            pltpu.VMEM((ff, half), bf16),
            pltpu.VMEM((NZ, n_rows, ff), f32),
            pltpu.VMEM((NZ, n_rows, ff), bf16),
        ),
        in_specs=[hbm] * 5,
        out_specs=(vmem,) * 4,
        scratch_shapes=[
            pltpu.VMEM((2, tok), f32),
            pltpu.VMEM((2, tok), jnp.int32),
            pltpu.VMEM((2, NZ, NY, tok, GATE + width), bf16),
            pltpu.VMEM((2, NZ, n_rows, ff), bf16),
            pltpu.VMEM((len(PAIRS), 4 * n_rows, ff), bf16),
            pltpu.VMEM((ff, width), bf16),
            pltpu.VMEM((ff, half), f32),
            pltpu.VMEM((NZ, n_rows, ff), bf16),
            pltpu.VMEM((ff, half), bf16),
            pltpu.SemaphoreType.DMA((7,)),
            pltpu.SemaphoreType.DMA((N_COPIES,)),
            pltpu.SemaphoreType.DMA((N_COPIES,)),
        ],
        compiler_params=pltpu.CompilerParams(collective_id=0, has_side_effects=True, vmem_limit_bytes=32 * 2**20),
    )(*(pltpu.with_memory_space_constraint(x, pltpu.HBM) for x in operands))
    gh, gw = pl.pallas_call(
        finish,
        out_shape=(jax.ShapeDtypeStruct((NZ, n_rows, ff), bf16), jax.ShapeDtypeStruct((ff, half), f32)),
        in_specs=[vmem] * 4,
        out_specs=(hbm, hbm),
        scratch_shapes=[
            pltpu.VMEM((NZ, n_rows, ff), bf16),
            pltpu.VMEM((ff, half), f32),
            pltpu.SemaphoreType.DMA((5,)),
        ],
        compiler_params=pltpu.CompilerParams(vmem_limit_bytes=16 * 2**20),
    )(*halves)
    return gh.reshape(1, 1, cap // 2, ff), gw.reshape(1, ff, half)


def solution(mesh):
    in_specs = (
        P("dp", ("expert", "ff"), "mp"),
        P("dp", ("expert", "ff"), None),
        P("dp", ("expert", "ff"), None),
        P("dp", "expert", None, "ff"),
        P("expert", "ff", "mp"),
    )
    out_specs = (P("dp", "expert", "mp", "ff"), P("expert", "ff", ("mp", "dp")))
    return jax.shard_map(body, mesh=mesh, in_specs=in_specs, out_specs=out_specs, check_vma=False)
```

time: 151 us -> 44.3 us (0.29)
  blocking collectives: 86.2 us -> 0 us
  Pallas kernels: 0 us -> 43.5 us
  waiting for transfers between devices: 37.5 us -> 0 us
  between operations: 14.1 us -> 0.64 us
  matrix products: 5.82 us -> 0 us
  local copies, waits for them, and re-layouts: 5.16 us -> 0 us
  other arithmetic: 2.17 us -> 0 us
    all_to_all x1 -> x0, blocking collectives: 86.2 us -> none  [body(): lax.all_to_all(copies, ('expert', 'ff'), split_axis=0, concat_axis=0, til...]
    pallas_call x0 -> x2, Pallas kernels: none -> 43.5 us  [the longest x1 42.4 us: body(): pl.pallas_call(kernel, out_shape=(pltpu.VMEM((ff, half), f32), pltpu.VMEM...]
    reduce_scatter x2 -> x0, waiting for transfers between devices: 37.4 us -> none  [the longest x1 20.2 us: body(): lax.psum_scatter(lax.dot_general(routed, weight_local, (((1,), (1,)), (()...]
    dot_general x3 -> x0, matrix products: 5.82 us -> none  [the longest x1 3.69 us: body(): lax.dot_general(routed, weight_local, (((1,), (1,)), ((), ())), preferred...]
    unnamed x9 -> x0, local copies, waits for them, and re-layouts: 4.41 us -> none
  transfers between devices with their start and end apart: 2 -> 0, of which waited for: 2 -> 0; matrix products, arithmetic and copies ran while one was open for 4% -> 0% of each run, Pallas kernels for 0% -> 0%
where the time goes in v2:
time: 44.3 us; the launch traced here: 44.1 us
  Pallas kernels  43.5 us (98%)
  between operations  0.64 us (1%)
    pallas_call x1, Pallas kernels, body(): pl.pallas_call(kernel, out_shape=(pltpu.VMEM((ff, half), f32), pltpu.VMEM...  42.4 us
    pallas_call x1, Pallas kernels, body(): pl.pallas_call(finish, out_shape=(jax.ShapeDtypeStruct((NZ, n_rows, ff),...  1.05 us

profile of v2, /device:TPU:1, one launch (start us, length us, event | category | flops | bytes accessed | tf_op | source)
XLA Modules:
  0.0 44.1 jit_solution(7926022586307682265)
XLA Ops:
  0.6 42.4 %shard_map.68 = (f32[256,768]{1,0:T(8,128)S(1)}, bf16[256,768]{1,0:T(8,128)(2,1)S(1)}, f32[8,64,256]{2,1,0:T(8,128)S(1)}, bf16[8,64,256]{2,1,0:T(8,128)(2,1)S(1)}) custom-call(bf16[16,1536]{1,0:T(8,128)(2,1)} %bitcast.13, f32[2,16]{1,0:T(2,128)} %bitcast.14, s32[2,16]{1,0:T(2,128)} %bitcast.15, bf16[2,8,64,256]{3,2,1,0:T(8,128)(2,1)} %bitcast.12, ...), custom_call_target="tpu_custom_call" | custom-call | tf_op jit(solution)/shard_map/pallas_call | solution.py:266
  43.0 1.0 %shard_map.69 = (bf16[8,64,256]{2,1,0:T(8,128)(2,1)}, f32[256,768]{1,0:T(8,128)}) custom-call(f32[256,768]{1,0:T(8,128)S(1)} %get-tuple-element.8.acc_k, bf16[256,768]{1,0:T(8,128)(2,1)S(1)} %get-tuple-element.9.gw_got, f32[8,64,256]{2,1,0:T(8,128)S(1)} %get-tuple-element.10.gh_keep, bf16[8,64,256]{2,1,0:T(8,128)(2,1)S(1)} %get-tuple-element.11.gh_got), custom_call_target="tpu_custom_call" | custom-call | tf_op jit(solution)/shard_map/pallas_call | solution.py:292

commit v3 on v2

--- a/solution.py
+++ b/solution.py
@@ -1,3 +1,5 @@
+import functools
+
 import jax
 import jax.numpy as jnp
 from jax import lax
@@ -8,26 +10,92 @@
 MESH = pl.DeviceIdType.MESH
 NY, NZ = 4, 8
 GATE = 128
-SPLITS = (384, 256)
+SPLITS = (256, 256)
 YS = (1, 3, 2)
 NEAR = (2, -2, 1, -1)
+ALL = (2, -2, 1, -1, 3, -3, 4)
+REACH = ((ALL, ALL), (ALL, NEAR))
 PAIRS = ((0, 1), (-1, 2), (-2, 3), (-3, 4))
 STEP = 256
-N_COPIES = 2 * (3 + 4 + 3 + 7 + 3 * NZ + 2 * NZ) + NZ + 8
+N_COPIES = 2 * (3 + 7 + 7 + 3 * NZ + 2 * NZ) + NZ + 3
+
+
+ORDERS = ((
+    ("start", 0),
+    ("a_near", 0),
+    ("b_near", 0),
+    ("share", 0, (0,)),
+    ("start", 1),
+    ("share", 0, (-2, 2, -1, 1)),
+    ("share", 0, (-3, 3, 4)),
+    ("a_near", 1),
+    ("b_near", 1),
+    ("receive", 0, PAIRS[0]),
+    ("s", 0),
+    ("receive", 0, PAIRS[1]),
+    ("s", 1),
+    ("receive", 0, PAIRS[2]),
+    ("s", 2),
+    ("receive", 0, PAIRS[3]),
+    ("s", 3),
+    ("share", 1, (0,)),
+    ("share", 1, (-2, 2, -1, 1)),
+    ("receive", 1, PAIRS[0]),
+    ("k", 0),
+    ("receive", 1, PAIRS[1]),
+    ("k", 1),
+    ("share", 1, (-3, 3, 4)),
+    ("receive", 1, PAIRS[2]),
+    ("k", 2),
+    ("receive", 1, PAIRS[3]),
+    ("k", 3),
+), (
+    ("start", 0),
+    ("a_near", 0),
+    ("b_near", 0),
+    ("share", 0, (0,)),
+    ("start", 1),
+    ("share", 0, (-2, 2, -1, 1)),
+    ("share", 0, (-3, 3, 4)),
+    ("a_near", 1),
+    ("b_near", 1),
+    ("receive", 0, PAIRS[0]),
+    ("s", 0),
+    ("receive", 0, PAIRS[1]),
+    ("s", 1),
+    ("receive", 0, PAIRS[2]),
+    ("s", 2),
+    ("receive", 0, PAIRS[3]),
+    ("s", 3),
+    ("a_far", 1),
+    ("b_far", 1),
+    ("share", 1, (0,)),
+    ("share", 1, (-2, 2, -1, 1)),
+    ("receive", 1, PAIRS[0]),
+    ("k", 0),
+    ("receive", 1, PAIRS[1]),
+    ("k", 1),
+    ("share", 1, (-3, 3, 4)),
+    ("receive", 1, PAIRS[2]),
+    ("k", 2),
+    ("receive", 1, PAIRS[3]),
+    ("k", 3),
+))
 
 
 def kernel(tok_hbm, gate_hbm, route_hbm, hid_hbm, w_hbm, acc_k, gw_got, gh_keep, gh_got,
            gate_ref, route_ref, rows, hid, scaled, w, acc_s, gh_send, gw_send, in_sem, send_sem, recv_sem):
     dp, e, f, mp = (lax.axis_index(a) for a in ("dp", "expert", "ff", "mp"))
-    y, z = lax.rem(f, NY), f // NY
+    y, z = f & (NY - 1), f // NY
+    ys, zs = [(y + k) & (NY - 1) for k in range(NY)], [(z + k) & (NZ - 1) for k in range(NZ)]
     width = w.shape[1]
     half = width // 2
 
     def dev(dy=0, dz=0):
-        return (dp, e, lax.rem(z + dz + NZ, NZ) * NY + lax.rem(y + dy + NY, NY), mp)
+        return (dp, e, zs[dz % NZ] * NY + ys[dy % NY], mp)
 
     def plane(d):
-        return lax.rem(z + d + NZ, NZ)
+        return zs[d % NZ]
 
     sibling, across, pair = (dp, 1 - e, f, mp), (1 - dp, e, f, mp), (dp, e, f, 1 - mp)
 
@@ -48,13 +116,12 @@
     for load in loads:
         load.start()
     barrier = pltpu.get_barrier_semaphore()
-    partners = [dev(dy=k) for k in YS] + [dev(dz=d) for d in NEAR] + [sibling, across, pair]
+    around = [dev(dy=k) for k in YS] + [dev(dz=d) for d in ALL]
+    partners = [sibling, across, pair, *around]
     for p in partners:
         pl.semaphore_signal(barrier, inc=1, device_id=p, device_id_type=MESH)
     for load in later:
         load.start()
-    acc_s[...] = jnp.zeros_like(acc_s)
-    acc_k[...] = jnp.zeros_like(acc_k)
 
     tok = rows.shape[3]
     diag = lax.broadcasted_iota(jnp.int32, (tok, tok), 0) == lax.broadcasted_iota(jnp.int32, (tok, tok), 1)
@@ -70,89 +137,96 @@
     rows[e, z, y, :, pl.ds(0, GATE)] = block.astype(jnp.bfloat16)
     loads[0].wait()
     loads[1].wait()
-    pl.semaphore_wait(barrier, len(partners))
-
-    sent = []
-
-    def send(src, dst, to):
-        i = len(sent)
-        copy = pltpu.make_async_remote_copy(
+    numbers = {}
+
+    def copy(key, src, dst, to):
+        i = numbers.setdefault(key, len(numbers))
+        return pltpu.make_async_remote_copy(
             src_ref=src, dst_ref=dst, send_sem=send_sem.at[i], recv_sem=recv_sem.at[i], device_id=to, device_id_type=MESH
         )
-        copy.start()
-        sent.append(copy)
-        return copy
+
+    def send(key, src, dst, to):
+        c = copy(key, src, dst, to)
+        c.start()
+        sent.append(c)
+        return c
 
     def wait(copies):
-        for copy in copies:
-            copy.wait_recv()
+        for c in copies:
+            c.wait_recv()
+
+    spans = (pl.ds(0, GATE + half), pl.ds(GATE + half, half))
 
     class Gather:
-        def __init__(self, start, size, first):
-            self.a, self.b = pl.ds(start, first), pl.ds(start + first, size - first)
-            self.sib = {}
+        def __init__(self, core, n):
+            self.n, self.reach = n, REACH[core][n]
+            at = spans[n]
+            self.a, self.b = pl.ds(at.start, SPLITS[n]), pl.ds(at.start + SPLITS[n], at.size - SPLITS[n])
 
         def a_plane(self, d, dz):
             ref = rows.at[e, plane(d), :, :, self.a]
-            return send(ref, ref, dev(dz=dz))
+            return send(("a_z", self.n, (d - dz) % NZ), ref, ref, dev(dz=dz))
 
         def b_block(self, d, dy=0, dz=0):
             ref = rows.at[e, plane(d), y, :, self.b]
-            return send(ref, ref, dev(dy=dy, dz=dz))
+            key = ("b_y", self.n, d % NZ, dy) if dy else ("b_z", self.n, (d - dz) % NZ)
+            return send(key, ref, ref, dev(dy=dy, dz=dz))
 
         def spread(self, d):
-            self.b_y[d] = [self.b_block(d, dy=k) for k in YS]
+            self.b_y[d % NZ] = [self.b_block(d, dy=k) for k in YS]
 
         def start(self):
             ref = rows.at[e, z, y, :, self.a]
-            self.a_y = [send(ref, ref, dev(dy=k)) for k in YS]
-            self.b_z = {-dz: self.b_block(0, dz=dz) for dz in NEAR}
+            self.a_y = [send(("a_y", self.n, k), ref, ref, dev(dy=k)) for k in YS]
+            self.b_z = {-dz % NZ: self.b_block(0, dz=dz) for dz in self.reach}
             self.b_y = {}
             self.spread(0)
 
         def a_near(self):
             wait(self.a_y)
-            self.a_z = {-dz: self.a_plane(0, dz) for dz in NEAR}
-
-        def b_far(self):
-            self.b_z[-2].wait_recv()
-            self.b_z[-3] = self.b_block(-2, dz=1)
-            self.spread(-2)
-            self.b_z[2].wait_recv()
-            self.b_z[3] = self.b_block(2, dz=-1)
-            self.b_z[4] = self.b_block(2, dz=-2)
-            self.spread(2)
-            for d in (-1, 1):
-                self.b_z[d].wait_recv()
-                self.spread(d)
+            self.a_z = {-dz % NZ: self.a_plane(0, dz) for dz in self.reach}
+
+        def b_near(self):
+            for dz in self.reach:
+                self.b_z[-dz % NZ].wait_recv()
+                if len(self.reach) < NZ - 1:
+                    if dz == 2:
+                        self.b_z[5] = self.b_block(-2, dz=1)
+                    if dz == -2:
+                        self.b_z[3] = self.b_block(2, dz=-1)
+                        self.b_z[4] = self.b_block(2, dz=-2)
+                self.spread(-dz)
 
         def a_far(self):
-            self.a_z[-2].wait_recv()
-            self.a_z[-3] = self.a_plane(-2, 1)
+            self.a_z[6].wait_recv()
+            self.a_z[5] = self.a_plane(-2, 1)
             self.a_z[4] = self.a_plane(-2, 2)
             self.a_z[2].wait_recv()
             self.a_z[3] = self.a_plane(2, -1)
 
-        def b_last(self):
+        def b_far(self):
             for d in (-3, 3, 4):
-                self.b_z[d].wait_recv()
+                self.b_z[d % NZ].wait_recv()
                 self.spread(d)
 
-        def share_a(self, ds):
+        def shared(self, part, d):
+            ref = rows.at[e, plane(d), :, :, self.a if part == "a" else self.b]
+            return ("share", part, self.n, d), ref, ref, sibling
+
+        def share(self, ds):
             for d in ds:
-                if d not in (0, 2, -2):
-                    self.a_z[d].wait_recv()
-                ref = rows.at[e, plane(d), :, :, self.a]
-                self.sib.setdefault(d, []).append(send(ref, ref, sibling))
-
-        def share_b(self, ds):
+                if d and not (d in (2, -2) and len(self.reach) < NZ - 1):
+                    self.a_z[d % NZ].wait_recv()
+                send(*self.shared("a", d))
+                wait(self.b_y[d % NZ])
+                send(*self.shared("b", d))
+
+        def receive(self, ds):
             for d in ds:
-                wait(self.b_y[d])
-                ref = rows.at[e, plane(d), :, :, self.b]
-                self.sib.setdefault(d, []).append(send(ref, ref, sibling))
+                for part in "ab":
+                    copy(*self.shared(part, d)).wait_recv()
 
     n_rows = NY * tok
-    gh_sends, gw_sends = [], []
 
     def take(ds, at):
         parts = [rows[c, plane(d), :, :, at].reshape(n_rows, -1) for c in (mp, 1 - mp) for d in ds]
@@ -166,12 +240,10 @@
     def grow(i, ds, acc, start, n):
         x = take(ds, pl.ds(start + n, STEP))
         more = lax.dot_general(scaled[i], x, (((0,), (0,)), ((), ())), preferred_element_type=jnp.float32)
-        return acc[:, n:n + STEP] + more
+        return acc[:, n:n + STEP] + more if i else more
 
     def compute_s(i):
         ds = PAIRS[i]
-        for d in ds:
-            wait(first.sib[d])
         h = jnp.concatenate([hid[c, plane(d)] for c in (mp, 1 - mp) for d in ds], axis=0)
         scaled[i] = (h.astype(jnp.float32) * gate_of(ds)).astype(jnp.bfloat16)
         for n in range(0, half, STEP):
@@ -179,61 +251,41 @@
             if i == len(PAIRS) - 1:
                 at = pl.ds(n, STEP)
                 gw_send[:, n:n + STEP] = total.astype(jnp.bfloat16)
-                gw_sends.append(send(gw_send.at[:, at], gw_got.at[:, at], across))
+                gw_sends.append(send(("gw", n), gw_send.at[:, at], gw_got.at[:, at], across))
             else:
                 acc_s[:, n:n + STEP] = total
 
     def compute_k(i):
         ds = PAIRS[i]
-        for d in ds:
-            wait(second.sib[d])
         x = take(ds, pl.ds(GATE, width))
         gh = lax.dot_general(x, w[...], (((1,), (1,)), ((), ())), preferred_element_type=jnp.float32) * gate_of(ds)
         for j, d in enumerate(ds):
             gh_send[plane(d)] = gh[(j + 2) * n_rows:(j + 3) * n_rows].astype(jnp.bfloat16)
-            gh_sends.append(send(gh_send.at[plane(d)], gh_got.at[plane(d)], pair))
+            gh_sends.append(send(("gh", d), gh_send.at[plane(d)], gh_got.at[plane(d)], pair))
             gh_keep[plane(d)] = gh[j * n_rows:(j + 1) * n_rows]
         for n in range(0, half, STEP):
             acc_k[:, n:n + STEP] = grow(i, ds, acc_k, GATE + half, n)
 
-    first, second = Gather(0, GATE + half, SPLITS[0]), Gather(GATE + half, half, SPLITS[1])
-    first.start()
-    first.a_near()
-    first.b_far()
-    second.start()
-    first.share_a((0,))
-    first.share_b((0,))
-    first.a_far()
-    first.b_last()
-    first.share_a((-2, 2, -1, 1))
-    first.share_b((-2, 2, -1, 1))
-    second.a_near()
-    second.b_far()
-    later[0].wait()
-    compute_s(0)
-    compute_s(1)
-    second.share_a((0,))
-    second.share_b((0,))
-    first.share_a((-3, 3, 4))
-    first.share_b((-3, 3, 4))
-    second.a_far()
-    second.b_last()
-    second.share_a((-2, 2, -1, 1))
-    second.share_b((-2, 2, -1, 1))
-    compute_s(2)
-    compute_s(3)
-    later[1].wait()
-    later[2].wait()
-    compute_k(0)
-    compute_k(1)
-    second.share_a((-3, 3, 4))
-    second.share_b((-3, 3, 4))
-    compute_k(2)
-    compute_k(3)
-    for copy in sent:
-        copy.wait_send()
-    wait(gh_sends)
-    wait(gw_sends)
+    def follow(order):
+        loaded = {"s": later[:1], "k": later[1:]}
+        for step, *args in order:
+            if step in loaded:
+                for load in loaded.pop(step):
+                    load.wait()
+            if step in "sk":
+                (compute_s if step == "s" else compute_k)(*args)
+            else:
+                getattr(gathers[args[0]], step)(*args[1:])
+        for c in sent:
+            c.wait_send()
+        wait(gh_sends)
+        wait(gw_sends)
+
+    pl.semaphore_wait(barrier, len(partners))
+    for core, order in enumerate(ORDERS):
+        gathers = [Gather(core, n) for n in range(2)]
+        sent, gh_sends, gw_sends = [], [], []
+        pl.when(e == core)(functools.partial(follow, order))
 
 
 def finish(acc_k, gw_got, gh_keep, gh_got, gh_hbm, gw_hbm, gh, gw, sem):

time: 44.3 us -> 42.1 us (0.950)
  Pallas kernels: 43.5 us -> 41.3 us
    pallas_call x1, Pallas kernels: 42.4 us -> 40.2 us  [body(): pl.pallas_call(kernel, out_shape=(pltpu.VMEM((ff, half), f32), pltpu.VMEM...]
where the time goes in v3:
time: 42.1 us; the launch traced here: 41.9 us
  Pallas kernels  41.3 us (98%)
  between operations  0.64 us (2%)
    pallas_call x1, Pallas kernels, body(): pl.pallas_call(kernel, out_shape=(pltpu.VMEM((ff, half), f32), pltpu.VMEM...  40.2 us
    pallas_call x1, Pallas kernels, body(): pl.pallas_call(finish, out_shape=(jax.ShapeDtypeStruct((NZ, n_rows, ff),...  1.05 us

profile of v3, /device:TPU:1, one launch (start us, length us, event | category | flops | bytes accessed | tf_op | source)
XLA Modules:
  0.0 41.9 jit_solution(4015626766657716334)
XLA Ops:
  0.6 40.2 %shard_map.68 = (f32[256,768]{1,0:T(8,128)S(1)}, bf16[256,768]{1,0:T(8,128)(2,1)S(1)}, f32[8,64,256]{2,1,0:T(8,128)S(1)}, bf16[8,64,256]{2,1,0:T(8,128)(2,1)S(1)}) custom-call(bf16[16,1536]{1,0:T(8,128)(2,1)} %bitcast.13, f32[2,16]{1,0:T(2,128)} %bitcast.14, s32[2,16]{1,0:T(2,128)} %bitcast.15, bf16[2,8,64,256]{3,2,1,0:T(8,128)(2,1)} %bitcast.12, ...), custom_call_target="tpu_custom_call" | custom-call | tf_op jit(solution)/shard_map/pallas_call | solution.py:318
  40.9 1.0 %shard_map.69 = (bf16[8,64,256]{2,1,0:T(8,128)(2,1)}, f32[256,768]{1,0:T(8,128)}) custom-call(f32[256,768]{1,0:T(8,128)S(1)} %get-tuple-element.8.acc_k, bf16[256,768]{1,0:T(8,128)(2,1)S(1)} %get-tuple-element.9.gw_got, f32[8,64,256]{2,1,0:T(8,128)S(1)} %get-tuple-element.10.gh_keep, bf16[8,64,256]{2,1,0:T(8,128)(2,1)S(1)} %get-tuple-element.11.gh_got), custom_call_target="tpu_custom_call" | custom-call | tf_op jit(solution)/shard_map/pallas_call | solution.py:344

commit v4 on v3

--- a/solution.py
+++ b/solution.py
@@ -15,70 +15,124 @@
 NEAR = (2, -2, 1, -1)
 ALL = (2, -2, 1, -1, 3, -3, 4)
 REACH = ((ALL, ALL), (ALL, NEAR))
-PAIRS = ((0, 1), (-1, 2), (-2, 3), (-3, 4))
+GROUPS = ((0,), (1, -1), (2, -2), (3, -3, 4))
 STEP = 256
-N_COPIES = 2 * (3 + 7 + 7 + 3 * NZ + 2 * NZ) + NZ + 3
+N_COPIES = 2 * (3 + 7 + 7 + 3 * NZ + 2 * NZ) + NZ + 4
 
 
 ORDERS = ((
     ("start", 0),
+    ("y_start", 1),
     ("a_near", 0),
     ("b_near", 0),
-    ("share", 0, (0,)),
-    ("start", 1),
-    ("share", 0, (-2, 2, -1, 1)),
-    ("share", 0, (-3, 3, 4)),
+    ("share", 0, "a", (0,)),
+    ("share", 0, "b", (0,)),
+    ("z_start", 1),
+    ("share", 1, "a", (0,)),
+    ("share", 1, "b", (0,)),
+    ("share", 0, "a", (-2,)),
+    ("share", 0, "b", (-2,)),
+    ("share", 0, "a", (2,)),
+    ("share", 0, "b", (2,)),
+    ("share", 0, "a", (-1,)),
+    ("share", 0, "b", (-1,)),
+    ("share", 0, "a", (1,)),
+    ("share", 0, "b", (1,)),
+    ("receive", 0, "ab", GROUPS[0]),
+    ("s", 0, "ab"),
+    ("receive", 1, "ab", GROUPS[0]),
+    ("k", 0),
+    ("share", 0, "a", (-3,)),
+    ("share", 0, "b", (-3,)),
+    ("share", 0, "a", (3,)),
+    ("share", 0, "b", (3,)),
+    ("share", 0, "a", (4,)),
+    ("share", 0, "b", (4,)),
     ("a_near", 1),
     ("b_near", 1),
-    ("receive", 0, PAIRS[0]),
-    ("s", 0),
-    ("receive", 0, PAIRS[1]),
-    ("s", 1),
-    ("receive", 0, PAIRS[2]),
-    ("s", 2),
-    ("receive", 0, PAIRS[3]),
-    ("s", 3),
-    ("share", 1, (0,)),
-    ("share", 1, (-2, 2, -1, 1)),
-    ("receive", 1, PAIRS[0]),
-    ("k", 0),
-    ("receive", 1, PAIRS[1]),
+    ("receive", 0, "ab", GROUPS[1]),
+    ("s", 1, "ab"),
+    ("receive", 0, "ab", GROUPS[2]),
+    ("s", 2, "ab"),
+    ("receive", 0, "ab", GROUPS[3]),
+    ("s", 3, "ab"),
+    ("share", 1, "a", (-2,)),
+    ("share", 1, "b", (-2,)),
+    ("share", 1, "a", (2,)),
+    ("share", 1, "b", (2,)),
+    ("share", 1, "a", (-1,)),
+    ("share", 1, "b", (-1,)),
+    ("share", 1, "a", (1,)),
+    ("share", 1, "b", (1,)),
+    ("receive", 1, "ab", GROUPS[1]),
     ("k", 1),
-    ("share", 1, (-3, 3, 4)),
-    ("receive", 1, PAIRS[2]),
+    ("receive", 1, "ab", GROUPS[2]),
     ("k", 2),
-    ("receive", 1, PAIRS[3]),
+    ("share", 1, "a", (-3,)),
+    ("share", 1, "b", (-3,)),
+    ("share", 1, "a", (3,)),
+    ("share", 1, "b", (3,)),
+    ("share", 1, "a", (4,)),
+    ("share", 1, "b", (4,)),
+    ("receive", 1, "ab", GROUPS[3]),
     ("k", 3),
 ), (
     ("start", 0),
+    ("y_start", 1),
     ("a_near", 0),
     ("b_near", 0),
-    ("share", 0, (0,)),
-    ("start", 1),
-    ("share", 0, (-2, 2, -1, 1)),
-    ("share", 0, (-3, 3, 4)),
+    ("share", 0, "a", (0,)),
+    ("share", 0, "b", (0,)),
+    ("z_start", 1),
+    ("share", 1, "a", (0,)),
+    ("share", 1, "b", (0,)),
+    ("share", 0, "a", (-2,)),
+    ("share", 0, "b", (-2,)),
+    ("share", 0, "a", (2,)),
+    ("share", 0, "b", (2,)),
+    ("share", 0, "a", (-1,)),
+    ("share", 0, "b", (-1,)),
+    ("share", 0, "a", (1,)),
+    ("share", 0, "b", (1,)),
+    ("receive", 0, "ab", GROUPS[0]),
+    ("s", 0, "ab"),
+    ("receive", 1, "ab", GROUPS[0]),
+    ("k", 0),
+    ("share", 0, "a", (-3,)),
+    ("share", 0, "b", (-3,)),
+    ("share", 0, "a", (3,)),
+    ("share", 0, "b", (3,)),
+    ("share", 0, "a", (4,)),
+    ("share", 0, "b", (4,)),
     ("a_near", 1),
     ("b_near", 1),
-    ("receive", 0, PAIRS[0]),
-    ("s", 0),
-    ("receive", 0, PAIRS[1]),
-    ("s", 1),
-    ("receive", 0, PAIRS[2]),
-    ("s", 2),
-    ("receive", 0, PAIRS[3]),
-    ("s", 3),
+    ("receive", 0, "ab", GROUPS[1]),
+    ("s", 1, "ab"),
+    ("receive", 0, "ab", GROUPS[2]),
+    ("s", 2, "ab"),
+    ("receive", 0, "ab", GROUPS[3]),
+    ("s", 3, "ab"),
     ("a_far", 1),
     ("b_far", 1),
-    ("share", 1, (0,)),
-    ("share", 1, (-2, 2, -1, 1)),
-    ("receive", 1, PAIRS[0]),
-    ("k", 0),
-    ("receive", 1, PAIRS[1]),
+    ("share", 1, "a", (-2,)),
+    ("share", 1, "b", (-2,)),
+    ("share", 1, "a", (2,)),
+    ("share", 1, "b", (2,)),
+    ("share", 1, "a", (-1,)),
+    ("share", 1, "b", (-1,)),
+    ("share", 1, "a", (1,)),
+    ("share", 1, "b", (1,)),
+    ("receive", 1, "ab", GROUPS[1]),
     ("k", 1),
-    ("share", 1, (-3, 3, 4)),
-    ("receive", 1, PAIRS[2]),
+    ("receive", 1, "ab", GROUPS[2]),
     ("k", 2),
-    ("receive", 1, PAIRS[3]),
+    ("share", 1, "a", (-3,)),
+    ("share", 1, "b", (-3,)),
+    ("share", 1, "a", (3,)),
+    ("share", 1, "b", (3,)),
+    ("share", 1, "a", (4,)),
+    ("share", 1, "b", (4,)),
+    ("receive", 1, "ab", GROUPS[3]),
     ("k", 3),
 ))
 
@@ -159,7 +213,7 @@
 
     class Gather:
         def __init__(self, core, n):
-            self.n, self.reach = n, REACH[core][n]
+            self.n, self.reach, self.b_y = n, REACH[core][n], {}
             at = spans[n]
             self.a, self.b = pl.ds(at.start, SPLITS[n]), pl.ds(at.start + SPLITS[n], at.size - SPLITS[n])
 
@@ -178,12 +232,23 @@
         def start(self):
             ref = rows.at[e, z, y, :, self.a]
             self.a_y = [send(("a_y", self.n, k), ref, ref, dev(dy=k)) for k in YS]
+            self.z_start()
+            self.spread(0)
+
+        def y_start(self):
+            ref = rows.at[e, z, y, :, self.a]
+            self.a_y = [send(("a_y", self.n, k), ref, ref, dev(dy=k)) for k in YS]
+            self.spread(0)
+
+        def z_start(self):
             self.b_z = {-dz % NZ: self.b_block(0, dz=dz) for dz in self.reach}
-            self.b_y = {}
-            self.spread(0)
+
+        def own_plane(self):
+            wait(self.a_y)
+            self.a_y = []
 
         def a_near(self):
-            wait(self.a_y)
+            self.own_plane()
             self.a_z = {-dz % NZ: self.a_plane(0, dz) for dz in self.reach}
 
         def b_near(self):
@@ -213,17 +278,19 @@
             ref = rows.at[e, plane(d), :, :, self.a if part == "a" else self.b]
             return ("share", part, self.n, d), ref, ref, sibling
 
-        def share(self, ds):
+        def share(self, part, ds):
             for d in ds:
-                if d and not (d in (2, -2) and len(self.reach) < NZ - 1):
+                if part == "b":
+                    wait(self.b_y[d % NZ])
+                elif d == 0:
+                    self.own_plane()
+                elif d and not (d in (2, -2) and len(self.reach) < NZ - 1):
                     self.a_z[d % NZ].wait_recv()
-                send(*self.shared("a", d))
-                wait(self.b_y[d % NZ])
-                send(*self.shared("b", d))
-
-        def receive(self, ds):
+                send(*self.shared(part, d))
+
+        def receive(self, parts, ds):
             for d in ds:
-                for part in "ab":
+                for part in parts:
                     copy(*self.shared(part, d)).wait_recv()
 
     n_rows = NY * tok
@@ -237,34 +304,47 @@
         lanes = lax.broadcasted_iota(jnp.int32, gates.shape, 1)
         return jnp.sum(jnp.where((lanes // 2) == e, gates, 0.0), axis=1, keepdims=True)
 
-    def grow(i, ds, acc, start, n):
-        x = take(ds, pl.ds(start + n, STEP))
-        more = lax.dot_general(scaled[i], x, (((0,), (0,)), ((), ())), preferred_element_type=jnp.float32)
-        return acc[:, n:n + STEP] + more if i else more
-
-    def compute_s(i):
-        ds = PAIRS[i]
+    def grow(i, ds, acc, start, at):
+        h = jnp.concatenate([scaled[plane(d), j] for j in range(2) for d in ds], axis=0)
+        x = take(ds, pl.ds(start + at.start, at.size))
+        more = lax.dot_general(h, x, (((0,), (0,)), ((), ())), preferred_element_type=jnp.float32)
+        return acc[:, at] + more if i else more
+
+    def scale(i):
+        ds = GROUPS[i]
         h = jnp.concatenate([hid[c, plane(d)] for c in (mp, 1 - mp) for d in ds], axis=0)
-        scaled[i] = (h.astype(jnp.float32) * gate_of(ds)).astype(jnp.bfloat16)
-        for n in range(0, half, STEP):
-            total = grow(i, ds, acc_s, GATE, n)
-            if i == len(PAIRS) - 1:
-                at = pl.ds(n, STEP)
-                gw_send[:, n:n + STEP] = total.astype(jnp.bfloat16)
+        h = (h.astype(jnp.float32) * gate_of(ds)).astype(jnp.bfloat16)
+        for j in range(2):
+            for k, d in enumerate(ds):
+                at = (j * len(ds) + k) * n_rows
+                scaled[plane(d), j] = h[at:at + n_rows]
+
+    def compute_s(i, part):
+        if part != "b":
+            scale(i)
+        first = SPLITS[0] - GATE
+        start, stop = {"a": (0, first), "b": (first, half), "ab": (0, half)}[part]
+        for n in range(start, stop, STEP):
+            at = pl.ds(n, min(STEP, stop - n))
+            total = grow(i, GROUPS[i], acc_s, GATE, at)
+            if i == len(GROUPS) - 1:
+                gw_send[:, at] = total.astype(jnp.bfloat16)
                 gw_sends.append(send(("gw", n), gw_send.at[:, at], gw_got.at[:, at], across))
             else:
-                acc_s[:, n:n + STEP] = total
+                acc_s[:, at] = total
 
     def compute_k(i):
-        ds = PAIRS[i]
+        ds = GROUPS[i]
         x = take(ds, pl.ds(GATE, width))
         gh = lax.dot_general(x, w[...], (((1,), (1,)), ((), ())), preferred_element_type=jnp.float32) * gate_of(ds)
         for j, d in enumerate(ds):
-            gh_send[plane(d)] = gh[(j + 2) * n_rows:(j + 3) * n_rows].astype(jnp.bfloat16)
+            at = (j + len(ds)) * n_rows
+            gh_send[plane(d)] = gh[at:at + n_rows].astype(jnp.bfloat16)
             gh_sends.append(send(("gh", d), gh_send.at[plane(d)], gh_got.at[plane(d)], pair))
             gh_keep[plane(d)] = gh[j * n_rows:(j + 1) * n_rows]
         for n in range(0, half, STEP):
-            acc_k[:, n:n + STEP] = grow(i, ds, acc_k, GATE + half, n)
+            at = pl.ds(n, STEP)
+            acc_k[:, at] = grow(i, ds, acc_k, GATE + half, at)
 
     def follow(order):
         loaded = {"s": later[:1], "k": later[1:]}
@@ -330,7 +410,7 @@
             pltpu.VMEM((2, tok), jnp.int32),
             pltpu.VMEM((2, NZ, NY, tok, GATE + width), bf16),
             pltpu.VMEM((2, NZ, n_rows, ff), bf16),
-            pltpu.VMEM((len(PAIRS), 4 * n_rows, ff), bf16),
+            pltpu.VMEM((NZ, 2, n_rows, ff), bf16),
             pltpu.VMEM((ff, width), bf16),
             pltpu.VMEM((ff, half), f32),
             pltpu.VMEM((NZ, n_rows, ff), bf16),

time: 42.1 us -> 41.6 us (0.988)
  Pallas kernels: 41.3 us -> 40.8 us
    pallas_call x1, Pallas kernels: 40.2 us -> 39.7 us  [body(): pl.pallas_call(kernel, out_shape=(pltpu.VMEM((ff, half), f32), pltpu.VMEM...]
where the time goes in v4:
time: 41.6 us; the launch traced here: 41.4 us
  Pallas kernels  40.8 us (98%)
  between operations  0.64 us (2%)
    pallas_call x1, Pallas kernels, body(): pl.pallas_call(kernel, out_shape=(pltpu.VMEM((ff, half), f32), pltpu.VMEM...  39.7 us
    pallas_call x1, Pallas kernels, body(): pl.pallas_call(finish, out_shape=(jax.ShapeDtypeStruct((NZ, n_rows, ff),...  1.05 us

profile of v4, /device:TPU:1, one launch (start us, length us, event | category | flops | bytes accessed | tf_op | source)
XLA Modules:
  0.0 41.4 jit_solution(3820713716433691753)
XLA Ops:
  0.6 39.7 %shard_map.68 = (f32[256,768]{1,0:T(8,128)S(1)}, bf16[256,768]{1,0:T(8,128)(2,1)S(1)}, f32[8,64,256]{2,1,0:T(8,128)S(1)}, bf16[8,64,256]{2,1,0:T(8,128)(2,1)S(1)}) custom-call(bf16[16,1536]{1,0:T(8,128)(2,1)} %bitcast.13, f32[2,16]{1,0:T(2,128)} %bitcast.14, s32[2,16]{1,0:T(2,128)} %bitcast.15, bf16[2,8,64,256]{3,2,1,0:T(8,128)(2,1)} %bitcast.12, ...), custom_call_target="tpu_custom_call" | custom-call | tf_op jit(solution)/shard_map/pallas_call | solution.py:398
  40.3 1.0 %shard_map.69 = (bf16[8,64,256]{2,1,0:T(8,128)(2,1)}, f32[256,768]{1,0:T(8,128)}) custom-call(f32[256,768]{1,0:T(8,128)S(1)} %get-tuple-element.8.acc_k, bf16[256,768]{1,0:T(8,128)(2,1)S(1)} %get-tuple-element.9.gw_got, f32[8,64,256]{2,1,0:T(8,128)S(1)} %get-tuple-element.10.gh_keep, bf16[8,64,256]{2,1,0:T(8,128)(2,1)S(1)} %get-tuple-element.11.gh_got), custom_call_target="tpu_custom_call" | custom-call | tf_op jit(solution)/shard_map/pallas_call | solution.py:424

commit v5 on v4

--- a/solution.py
+++ b/solution.py
@@ -137,8 +137,8 @@
 ))
 
 
-def kernel(tok_hbm, gate_hbm, route_hbm, hid_hbm, w_hbm, acc_k, gw_got, gh_keep, gh_got,
-           gate_ref, route_ref, rows, hid, scaled, w, acc_s, gh_send, gw_send, in_sem, send_sem, recv_sem):
+def kernel(tok_hbm, gate_hbm, route_hbm, hid_hbm, w_hbm, acc_k, gh_sum,
+           gw_got, gh_keep, gh_got, gate_ref, route_ref, rows, hid, scaled, w, acc_s, gh_send, gw_send, in_sem, send_sem, recv_sem):
     dp, e, f, mp = (lax.axis_index(a) for a in ("dp", "expert", "ff", "mp"))
     y, z = f & (NY - 1), f // NY
     ys, zs = [(y + k) & (NY - 1) for k in range(NY)], [(z + k) & (NZ - 1) for k in range(NZ)]
@@ -358,8 +358,10 @@
                 getattr(gathers[args[0]], step)(*args[1:])
         for c in sent:
             c.wait_send()
+        wait(gw_sends)
+        acc_k[...] = acc_k[...] + gw_got[...].astype(jnp.float32)
         wait(gh_sends)
-        wait(gw_sends)
+        gh_sum[...] = (gh_keep[...] + gh_got[...].astype(jnp.float32)).astype(jnp.bfloat16)
 
     pl.semaphore_wait(barrier, len(partners))
     for core, order in enumerate(ORDERS):
@@ -368,16 +370,10 @@
         pl.when(e == core)(functools.partial(follow, order))
 
 
-def finish(acc_k, gw_got, gh_keep, gh_got, gh_hbm, gw_hbm, gh, gw, sem):
-    gh[...] = (gh_keep[...] + gh_got[...].astype(jnp.float32)).astype(jnp.bfloat16)
-    outs = [pltpu.make_async_copy(gh, gh_hbm, sem.at[0])]
-    outs[0].start()
-    n = gw.shape[0] // 4
-    for i in range(4):
-        at = pl.ds(i * n, n)
-        gw[at] = acc_k[at] + gw_got[at].astype(jnp.float32)
-        outs.append(pltpu.make_async_copy(gw.at[at], gw_hbm.at[at], sem.at[i + 1]))
-        outs[-1].start()
+def store(gw, gh, gh_hbm, gw_hbm, sem):
+    outs = [pltpu.make_async_copy(gw, gw_hbm, sem.at[0]), pltpu.make_async_copy(gh, gh_hbm, sem.at[1])]
+    for out in outs:
+        out.start()
     for out in outs:
         out.wait()
 
@@ -399,13 +395,14 @@
         kernel,
         out_shape=(
             pltpu.VMEM((ff, half), f32),
+            pltpu.VMEM((NZ, n_rows, ff), bf16),
+        ),
+        in_specs=[hbm] * 5,
+        out_specs=(vmem,) * 2,
+        scratch_shapes=[
             pltpu.VMEM((ff, half), bf16),
             pltpu.VMEM((NZ, n_rows, ff), f32),
             pltpu.VMEM((NZ, n_rows, ff), bf16),
-        ),
-        in_specs=[hbm] * 5,
-        out_specs=(vmem,) * 4,
-        scratch_shapes=[
             pltpu.VMEM((2, tok), f32),
             pltpu.VMEM((2, tok), jnp.int32),
             pltpu.VMEM((2, NZ, NY, tok, GATE + width), bf16),
@@ -422,15 +419,11 @@
         compiler_params=pltpu.CompilerParams(collective_id=0, has_side_effects=True, vmem_limit_bytes=32 * 2**20),
     )(*(pltpu.with_memory_space_constraint(x, pltpu.HBM) for x in operands))
     gh, gw = pl.pallas_call(
-        finish,
+        store,
         out_shape=(jax.ShapeDtypeStruct((NZ, n_rows, ff), bf16), jax.ShapeDtypeStruct((ff, half), f32)),
-        in_specs=[vmem] * 4,
+        in_specs=[vmem] * 2,
         out_specs=(hbm, hbm),
-        scratch_shapes=[
-            pltpu.VMEM((NZ, n_rows, ff), bf16),
-            pltpu.VMEM((ff, half), f32),
-            pltpu.SemaphoreType.DMA((5,)),
-        ],
+        scratch_shapes=[pltpu.SemaphoreType.DMA((2,))],
         compiler_params=pltpu.CompilerParams(vmem_limit_bytes=16 * 2**20),
     )(*halves)
     return gh.reshape(1, 1, cap // 2, ff), gw.reshape(1, ff, half)

time: 41.6 us -> 41.5 us (level)
  no operation moved by 1% of the time
where the time goes in v5:
time: 41.5 us; the launch traced here: 41.4 us
  Pallas kernels  40.7 us (98%)
  between operations  0.64 us (2%)
    pallas_call x1, Pallas kernels, body(): pl.pallas_call(kernel, out_shape=(pltpu.VMEM((ff, half), f32), pltpu.VMEM...  39.7 us
    pallas_call x1, Pallas kernels, body(): pl.pallas_call(store, out_shape=(jax.ShapeDtypeStruct((NZ, n_rows, ff), b...  0.98 us

profile of v5, /device:TPU:1, one launch (start us, length us, event | category | flops | bytes accessed | tf_op | source)
XLA Modules:
  0.0 41.4 jit_solution(13228288875541465185)
XLA Ops:
  0.6 39.7 %shard_map.68 = (f32[256,768]{1,0:T(8,128)S(1)}, bf16[8,64,256]{2,1,0:T(8,128)(2,1)S(1)}) custom-call(bf16[16,1536]{1,0:T(8,128)(2,1)} %bitcast.13, f32[2,16]{1,0:T(2,128)} %bitcast.14, s32[2,16]{1,0:T(2,128)} %bitcast.15, bf16[2,8,64,256]{3,2,1,0:T(8,128)(2,1)} %bitcast.12, bf16[256,1536]{1,0:T(8,128)(2,1)} %bitcast.11), custom_call_target="tpu_custom_call" | custom-call | tf_op jit(solution)/shard_map/pallas_call | solution.py:394
  40.4 1.0 %shard_map.69 = (bf16[8,64,256]{2,1,0:T(8,128)(2,1)}, f32[256,768]{1,0:T(8,128)}) custom-call(f32[256,768]{1,0:T(8,128)S(1)} %get-tuple-element.6.gw, bf16[8,64,256]{2,1,0:T(8,128)(2,1)S(1)} %get-tuple-element.7.gh), custom_call_target="tpu_custom_call" | custom-call | tf_op jit(solution)/shard_map/pallas_call | solution.py:421
